TPU v7x, 128 devices: a whole 4x4x4 slice. The times are simulated.
128 devices in a mesh: rows: 128 (over x, z, y, core).
Axes of the slice: x: 4, y: 4, z: 4, core: 2. Of those that a mesh axis runs over, the one named last changes fastest.
Arguments:
- slab: bfloat16 [1048576, 1024], P('rows'), may hold values from -36 to 36, as said below
- test_matrix: bfloat16 [1024, 256], replicated, may hold values from -0.1875 to 0.1875
Outputs:
- basis: float32 [1048576, 256], P('rows')
- coefficients: float32 [256, 1024], replicated
- gram_factor: float32 [256, 256], replicated
Inputs may be any that keep to these rules, and one draw needn't show every extreme that they name: `slab`: Real-valued embeddings.
All inputs are finite; a program needn't handle non-finite values.
Results may differ from a plain program's by a relative error of at most 0.00035.
Values sent between devices are 32-bit elements; how exact they have to be, the bound alone decides.
A program may use at most 128 MiB of HBM per device.

v0:
```python
import jax
import jax.numpy as jnp
from jax import lax
from jax.sharding import PartitionSpec as P


def factor_pair(gram):
    lower = jnp.linalg.cholesky(gram)
    eye = jnp.eye(gram.shape[0], dtype=gram.dtype)
    return (lower, lax.linalg.triangular_solve(lower, eye, left_side=True, lower=True))


def row_gram(left):
    return lax.dot_general(left, left, (((0,), (0,)), ((), ())), precision=lax.Precision.HIGHEST)


def project_rows(factor, slab):
    upper = factor.astype(jnp.bfloat16)
    lower = (factor - upper.astype(jnp.float32)).astype(jnp.bfloat16)
    stacked = jnp.concatenate([upper, lower], axis=1)
    both = lax.dot_general(
        stacked, slab, (((0,), (0,)), ((), ())), preferred_element_type=jnp.float32
    )
    width = factor.shape[1]
    return both[:width] + both[width:]


def local(slab, test_matrix):
    total_rows = lax.axis_size("rows") * slab.shape[0]
    sketch = jnp.dot(slab, test_matrix, preferred_element_type=jnp.float32)
    gram = lax.psum(row_gram(sketch), "rows")
    lower, first_inverse = factor_pair(gram)
    gram_factor = lower / jnp.sqrt(jnp.float32(total_rows))
    first_basis = jnp.dot(sketch, first_inverse.T, precision=lax.Precision.HIGHEST)
    second_gram = lax.psum(row_gram(first_basis), "rows")
    unused_lower, second_inverse = factor_pair(second_gram)
    orthonormal = jnp.dot(first_basis, second_inverse.T, precision=lax.Precision.HIGHEST)
    coefficients = lax.psum(project_rows(orthonormal, slab), "rows")
    basis = orthonormal * jnp.sqrt(jnp.float32(total_rows))
    return (basis, coefficients, gram_factor)


def solution(mesh):
    placed = (P("rows", None), P())
    return jax.shard_map(
        local, mesh=mesh, in_specs=placed, out_specs=(P("rows", None), P(), P()), check_vma=False
    )
```

profile of v0, /device:TPU:1, one launch (start us, length us, event | category | flops | bytes accessed | tf_op | source)
XLA Modules:
  0.0 653.6 jit_solution(13244283652427183121)
XLA Ops:
  8.2 8.3 %fusion.37 = f32[8192,256]{1,0:T(8,128)S(1)} fusion(bf16[8192,1024]{1,0:T(8,128)(2,1)} %param.5, bf16[1024,256]{1,0:T(8,128)(2,1)S(1)} %copy-done), kind=kOutput, calls=%fused_computation.74 | convolution fusion | flops 4294967296 | bytes 25690112 | tf_op jit(solution)/shard_map/dot_general | solution.py:30
  16.6 3.4 copy-done.3
  20.0 14.4 %fusion.38 = f32[256,256]{0,1:T(8,128)} fusion(f32[8192,256]{1,0:T(8,128)S(1)} %fusion.37), kind=kOutput, calls=%fused_computation.75 | convolution fusion | flops 6442450944 | bytes 8650752 | tf_op jit(solution)/shard_map/dot_general | solution.py:14
  34.5 144.8 %all-reduce.5.cloned.1.call-done = f32[256,256]{0,1:T(8,128)} async-done(((f32[256,256]{0,1:T(8,128)}), f32[256,256]{0,1:T(8,128)}) %all-reduce.5.cloned.1.call-update) | async-done | bytes 262160 | tf_op jit(solution)/shard_map/psum | solution.py:31
  181.4 11.7 %cholesky.130 = f32[128,128]{1,0:T(8,128)S(1)} custom-call(f32[128,128]{1,0:T(8,128)S(1)} %cholesky.194), custom_call_target="Cholesky" | custom-call | tf_op jit(solution)/shard_map/jit(cholesky)/cholesky | solution.py:8
  193.2 9.8 %custom-call.13 = f32[1,128,128]{1,2,0:T(8,128)S(1)} custom-call(f32[1,128,128]{2,1,0:T(8,128)S(1)} %get-tuple-element.56), custom_call_target="InvertDiagBlocksLowerTriangular" | custom-call | tf_op jit(solution)/shard_map/jit(cholesky)/cholesky | solution.py:8
  203.5 11.7 %cholesky.147 = f32[128,128]{1,0:T(8,128)S(1)} custom-call(f32[128,128]{1,0:T(8,128)S(1)} %convolution_subtract_fusion.3), custom_call_target="Cholesky" | custom-call | tf_op jit(solution)/shard_map/jit(cholesky)/cholesky | solution.py:8
  218.1 4.1 while.4
  222.2 19.7 %custom-call.14 = f32[2,128,128]{1,2,0:T(8,128)S(1)} custom-call(f32[2,128,128]{2,1,0:T(8,128)S(1)} %get-tuple-element.19), custom_call_target="InvertDiagBlocksLowerTriangular" | custom-call | tf_op jit(solution)/shard_map/triangular_solve/custom-call.0 | solution.py:10
  242.8 9.8 %fusion.4 = f32[8192,256]{1,0:T(8,128)S(1)} fusion(f32[8192,256]{1,0:T(8,128)} %copy-done.3, f32[128,256]{1,0:T(8,128)S(1)} %fusion.27, f32[128,256]{1,0:T(8,128)S(1)} %fusion.20), kind=kOutput, calls=%fused_computation.16 | convolution fusion | flops 6442516480 | bytes 17039360 | tf_op jit(solution)/shard_map/dot_general | solution.py:34
  252.6 3.4 copy-done.2
  256.0 14.6 %fusion.39 = f32[256,256]{0,1:T(8,128)} fusion(f32[8192,256]{1,0:T(8,128)S(1)} %fusion.4), kind=kOutput, calls=%fused_computation.76 | convolution fusion | flops 6442450944 | bytes 8650752 | tf_op jit(solution)/shard_map/dot_general | solution.py:14
  270.6 139.1 %all-reduce.7.cloned.1.call-done = f32[256,256]{0,1:T(8,128)} async-done(((f32[256,256]{0,1:T(8,128)}), f32[256,256]{0,1:T(8,128)}) %all-reduce.7.cloned.1.call-update) | async-done | bytes 262160 | tf_op jit(solution)/shard_map/psum | solution.py:35
  411.8 11.7 %cholesky.164 = f32[128,128]{1,0:T(8,128)S(1)} custom-call(f32[128,128]{1,0:T(8,128)S(1)} %cholesky.197), custom_call_target="Cholesky" | custom-call | tf_op jit(solution)/shard_map/jit(cholesky)/cholesky | solution.py:8
  424.2 9.8 %custom-call.15 = f32[1,128,128]{1,2,0:T(8,128)S(1)} custom-call(f32[1,128,128]{2,1,0:T(8,128)S(1)} %get-tuple-element.52), custom_call_target="InvertDiagBlocksLowerTriangular" | custom-call | tf_op jit(solution)/shard_map/jit(cholesky)/cholesky | solution.py:8
  434.6 11.7 %cholesky.181 = f32[128,128]{1,0:T(8,128)S(1)} custom-call(f32[128,128]{1,0:T(8,128)S(1)} %convolution_subtract_fusion.2), custom_call_target="Cholesky" | custom-call | tf_op jit(solution)/shard_map/jit(cholesky)/cholesky | solution.py:8
  448.4 4.4 while.5
  449.3 1.4 bitcast_dynamic-update-slice_fusion.5
  452.8 19.7 %custom-call.16 = f32[2,128,128]{1,2,0:T(8,128)S(1)} custom-call(f32[2,128,128]{2,1,0:T(8,128)S(1)} %get-tuple-element.20), custom_call_target="InvertDiagBlocksLowerTriangular" | custom-call | tf_op jit(solution)/shard_map/triangular_solve/custom-call.0 | solution.py:10
  473.4 12.4 %subtract_convert_fusion = (bf16[8192,256]{0,1:T(8,128)(2,1)S(1)}, bf16[8192,256]{0,1:T(8,128)(2,1)S(1)}, f32[8192,256]{0,1:T(8,128)}) fusion(f32[8192,256]{1,0:T(8,128)} %copy-done.2, f32[128,256]{1,0:T(8,128)S(1)} %fusion.23, f32[128,256]{1,0:T(8,128)S(1)} %fusion.18), kind=kOutput, calls=%fused_computation.8 | convolution fusion | flops 6453002240 | bytes 25427968 | tf_op jit(solution)/shard_map/dot_general | solution.py:37
  485.8 12.5 %fusion = f32[512,1024]{1,0:T(8,128)S(1)} fusion(bf16[8192,1024]{1,0:T(8,128)(2,1)} %param.5, bf16[8192,256]{0,1:T(8,128)(2,1)S(1)} %get-tuple-element.40, bf16[8192,256]{0,1:T(8,128)(2,1)S(1)} %get-tuple-element.41), kind=kOutput, calls=%fused_computation.4 | convolution fusion | flops 8606711808 | bytes 27262976 | tf_op jit(solution)/shard_map/dot_general | solution.py:21
  499.4 9.1 %copy.9 = f32[8192,256]{1,0:T(8,128)} copy(f32[8192,256]{0,1:T(8,128)} %get-tuple-element.46) | data formatting | bytes 16777216
  508.5 135.8 %all-reduce.9.cloned.1.call-done = f32[256,1024]{1,0:T(8,128)} async-done(((f32[256,1024]{1,0:T(8,128)}), f32[256,1024]{1,0:T(8,128)}) %all-reduce.9.cloned.1.call-update) | async-done | bytes 1048592 | tf_op jit(solution)/shard_map/psum | solution.py:38
  644.3 2.3 copy.37
  (56 shorter events, 18.9 us)
Async XLA Ops:
  7.2 1.1 copy-start
  7.2 172.1 %all-reduce.5.cloned.1.call-start = ((), (), s32[]{:S(2)}) async-start(), calls=%async_computation | async-start | bytes 524288 | tf_op jit(solution)/shard_map/psum | solution.py:31
  16.6 3.4 copy-start.3
  34.4 375.3 %all-reduce.7.cloned.1.call-start = ((), (), s32[]{:S(2)}) async-start(), calls=%async_computation.1 | async-start | bytes 524288 | tf_op jit(solution)/shard_map/psum | solution.py:35
  252.6 3.4 copy-start.2
  270.6 373.7 %all-reduce.9.cloned.1.call-start = ((), (), s32[]{:S(2)}) async-start(), calls=%async_computation.2 | async-start | bytes 2097152 | tf_op jit(solution)/shard_map/psum | solution.py:38
  499.4 147.2 %copy-start.1 = (bf16[1024,256]{1,0:T(8,128)(2,1)S(1)}, bf16[1024,256]{1,0:T(8,128)(2,1)}, u32[]{:S(2)}) copy-start(bf16[1024,256]{1,0:T(8,128)(2,1)} %param.6) | copy-start | bytes 1572868
Sparse Core Ops, SparseCore 0:
  34.5 144.7 all-reduce.4
  270.7 138.9 all-reduce.6
  499.5 144.7 all-reduce.8
where the time goes:
time: 657 us; the launch traced here: 654 us
  waiting for transfers between devices  420 us (64%)
  other arithmetic  112 us (17%)
  matrix products  74.7 us (11%)
  local copies, waits for them, and re-layouts  29.5 us (4%)
  between operations  17.1 us (3%)
    psum x1, waiting for transfers between devices, local(): gram = lax.psum(row_gram(sketch), 'rows')  145 us
    psum x1, waiting for transfers between devices, local(): second_gram = lax.psum(row_gram(first_basis), 'rows')  139 us
    psum x1, waiting for transfers between devices, local(): coefficients = lax.psum(project_rows(orthonormal, slab), 'rows')  136 us
    another operation x13, other arithmetic, factor_pair(): lower = jnp.linalg.cholesky(gram)  68.7 us
    another operation x4, other arithmetic, factor_pair(): lax.linalg.triangular_solve(lower, eye, left_side=True, lower=True)  39.4 us
    dot_general x2, matrix products, row_gram(): lax.dot_general(left, left, (((0,), (0,)), ((), ())), precision=lax.Preci...  29 us
    unnamed x10, local copies, waits for them, and re-layouts  19.2 us
  transfers between devices with their start and end apart: 3, of which 3 were waited for; matrix products, arithmetic and copies ran while one was open for 1% of the time, Pallas kernels for 0%

commit v1 on v0

v1 whole, which is shorter than its diff:
```python
import jax
import jax.numpy as jnp
from jax import lax
from jax.experimental import pallas as pl
from jax.experimental.pallas import tpu as pltpu
from jax.sharding import PartitionSpec as P

F32 = jnp.float32
HIGH = lax.Precision.HIGHEST
MESH = pl.DeviceIdType.MESH
NN = (((1,), (0,)), ((), ()))
NT = (((1,), (1,)), ((), ()))
TN = (((0,), (0,)), ((), ()))
CHIPS = 64
TILES = 32
PANEL = 64


def mul(left, right, dims=NN):
    return lax.dot_general(left, right, dims, precision=HIGH, preferred_element_type=F32)


def two_sum(a, b):
    total = a + b
    part = total - a
    return total, (a - (total - part)) + (b - part)


CHUNK = 1024


def sketch_kernel(slab_ref, test_ref, sketch_ref, gram_ref, proj_ref, low, cross):
    step = pl.program_id(0)

    @pl.when(step == 0)
    def _():
        gram_ref[...] = jnp.zeros_like(gram_ref)
        proj_ref[...] = jnp.zeros_like(proj_ref)
        low[...] = jnp.zeros_like(low)
        cross[...] = jnp.zeros_like(cross)

    block = slab_ref[...]
    sketch = jnp.dot(block, test_ref[...], preferred_element_type=F32)
    sketch_ref[...] = sketch
    turned = sketch.T

    most = jnp.max(jnp.abs(turned), axis=1, keepdims=True)
    magic = near_power(1.5 * most) * F32(1.5 * 2.0**16)
    one = (turned + magic) - magic
    rest = turned - one
    two = rest.astype(jnp.bfloat16)
    three = (rest - two.astype(F32)).astype(jnp.bfloat16)
    one = one.astype(jnp.bfloat16)

    def outer(left, right):
        return lax.dot_general(left, right, NT, preferred_element_type=F32)

    total, error = two_sum(gram_ref[...], outer(one, one))
    gram_ref[...] = total
    low[...] += error + outer(two, two)
    cross[...] += outer(one, two) + outer(one, three)

    upper = turned.astype(jnp.bfloat16)
    lower = (turned - upper.astype(F32)).astype(jnp.bfloat16)
    proj_ref[...] += jnp.dot(upper, block, preferred_element_type=F32) + jnp.dot(
        lower, block, preferred_element_type=F32)

    @pl.when(step == pl.num_programs(0) - 1)
    def _():
        mixed = cross[...]
        gram_ref[...] += (mixed + mixed.T) + low[...]


def sketch_all(slab, test_matrix):
    rows = slab.shape[0]
    return pl.pallas_call(
        sketch_kernel,
        grid=(rows // CHUNK,),
        out_shape=(
            jax.ShapeDtypeStruct((rows, 256), F32),
            jax.ShapeDtypeStruct((256, 256), F32),
            jax.ShapeDtypeStruct((256, 1024), F32),
        ),
        in_specs=[
            pl.BlockSpec((CHUNK, 1024), lambda i: (i, 0)),
            pl.BlockSpec((1024, 256), lambda i: (0, 0)),
        ],
        out_specs=(
            pl.BlockSpec((CHUNK, 256), lambda i: (i, 0)),
            pl.BlockSpec((256, 256), lambda i: (0, 0)),
            pl.BlockSpec((256, 1024), lambda i: (0, 0)),
        ),
        scratch_shapes=[pltpu.VMEM((256, 256), F32), pltpu.VMEM((256, 256), F32)],
        compiler_params=pltpu.CompilerParams(vmem_limit_bytes=40 * 2**20),
        name="sketch_all",
    )(slab, test_matrix)


def reduce_kernel(
    gram_ref, proj_ref, gram_out, proj_out,
    gram_pair, proj_pair, gram_half, proj_half, gram_slots, proj_slots,
    pair_send, pair_recv, part_send, part_recv, done_send, done_recv, last_send, last_recv,
):
    me = lax.axis_index("rows")
    chip = me // 2
    core = me % 2
    mate = chip * 2 + 1 - core
    other = 1 - core

    def peer(step):
        target = (chip + step) % CHIPS
        return target, target * 2 + core

    barrier = pltpu.get_barrier_semaphore()

    def greet(step, carry):
        _, device = peer(step)
        pl.semaphore_signal(barrier, inc=1, device_id=(device,), device_id_type=MESH)
        return carry

    lax.fori_loop(1, CHIPS, greet, 0)
    pl.semaphore_signal(barrier, inc=1, device_id=(mate,), device_id_type=MESH)
    pl.semaphore_wait(barrier, CHIPS)

    def rows_of(which, count):
        return pl.ds(pl.multiple_of(which * count, count), count)

    gram_swap = pltpu.make_async_remote_copy(
        src_ref=gram_ref.at[rows_of(other, 128)], dst_ref=gram_pair,
        send_sem=pair_send.at[0], recv_sem=pair_recv.at[0], device_id=(mate,), device_id_type=MESH)
    proj_swap = pltpu.make_async_remote_copy(
        src_ref=proj_ref.at[rows_of(other, 128)], dst_ref=proj_pair,
        send_sem=pair_send.at[1], recv_sem=pair_recv.at[1], device_id=(mate,), device_id_type=MESH)
    gram_swap.start()
    proj_swap.start()
    gram_swap.wait()
    gram_half[...] = gram_ref[rows_of(core, 128), :] + gram_pair[...]
    proj_swap.wait()
    proj_half[...] = proj_ref[rows_of(core, 128), :] + proj_pair[...]

    def tile_at(ref, index):
        return ref.at[
            pl.ds(pl.multiple_of((index // 2) * 8, 8), 8),
            pl.ds(pl.multiple_of((index % 2) * 128, 128), 128),
        ]

    def strip_of(index, base=0):
        return (
            pl.ds(pl.multiple_of(base + (index // 4) * 8, 8), 8),
            pl.ds(pl.multiple_of((index % 4) * 256, 256), 256),
        )

    def gram_part(target, device):
        return pltpu.make_async_remote_copy(
            src_ref=tile_at(gram_half, target), dst_ref=gram_slots.at[chip],
            send_sem=part_send.at[0], recv_sem=part_recv.at[0], device_id=(device,), device_id_type=MESH)

    def proj_part(target, device):
        return pltpu.make_async_remote_copy(
            src_ref=proj_half.at[strip_of(target)], dst_ref=proj_slots.at[chip],
            send_sem=part_send.at[1], recv_sem=part_recv.at[1], device_id=(device,), device_id_type=MESH)

    def scatter(step, carry):
        target, device = peer(step)

        @pl.when(target < TILES)
        def _():
            gram_part(target, device).start()

        proj_part(target, device).start()
        return carry

    lax.fori_loop(1, CHIPS, scatter, 0)
    owner = chip < TILES
    own_tile = chip % TILES

    gram_slots[chip] = tile_at(gram_half, own_tile)[...]
    proj_slots[chip] = proj_half[strip_of(chip)]

    def wait_bytes(ref, sem):
        pltpu.make_async_copy(ref, ref, sem).wait()

    gram_base = core * 128
    tile_rows = pl.ds(pl.multiple_of(gram_base + (own_tile // 2) * 8, 8), 8)
    tile_cols = pl.ds(pl.multiple_of((own_tile % 2) * 128, 128), 128)
    tile = gram_out.at[:, tile_rows, tile_cols]

    @pl.when(owner)
    def _():
        wait_bytes(gram_slots.at[pl.ds(0, CHIPS - 1)], part_recv.at[0])

        def add(index, pair):
            high, low = pair
            high, error = two_sum(high, gram_slots[index])
            return high, low + error

        high, low = lax.fori_loop(1, CHIPS, add, (gram_slots[0], jnp.zeros((8, 128), F32)))
        gram_out[0, tile_rows, tile_cols] = high
        gram_out[1, tile_rows, tile_cols] = low

        def share(step, carry):
            _, device = peer(step)
            pltpu.make_async_remote_copy(
                src_ref=tile, dst_ref=tile, send_sem=done_send.at[0], recv_sem=done_recv.at[0],
                device_id=(device,), device_id_type=MESH).start()
            return carry

        lax.fori_loop(1, CHIPS, share, 0)

    wait_bytes(proj_slots.at[pl.ds(0, CHIPS - 1)], part_recv.at[1])
    total = lax.fori_loop(
        1, CHIPS, lambda index, total: total + proj_slots[index], proj_slots[0])
    strip = strip_of(chip, core * 128)
    proj_out[strip] = total

    def share_proj(step, carry):
        _, device = peer(step)
        pltpu.make_async_remote_copy(
            src_ref=proj_out.at[strip], dst_ref=proj_out.at[strip],
            send_sem=done_send.at[1], recv_sem=done_recv.at[1],
            device_id=(device,), device_id_type=MESH).start()
        return carry

    lax.fori_loop(1, CHIPS, share_proj, 0)

    @pl.when(owner)
    def _():
        wait_bytes(gram_slots.at[pl.ds(0, 2 * (TILES - 1))], done_recv.at[0])

    @pl.when(jnp.logical_not(owner))
    def _():
        wait_bytes(gram_slots.at[pl.ds(0, 2 * TILES)], done_recv.at[0])

    gram_rows = rows_of(core, 128)
    gram_last = pltpu.make_async_remote_copy(
        src_ref=gram_out.at[:, gram_rows], dst_ref=gram_out.at[:, gram_rows],
        send_sem=last_send.at[0], recv_sem=last_recv.at[0], device_id=(mate,), device_id_type=MESH)
    gram_last.start()
    wait_bytes(proj_slots.at[pl.ds(0, CHIPS - 1)], done_recv.at[1])
    half_rows = rows_of(core, 128)
    proj_last = pltpu.make_async_remote_copy(
        src_ref=proj_out.at[half_rows], dst_ref=proj_out.at[half_rows],
        send_sem=last_send.at[1], recv_sem=last_recv.at[1], device_id=(mate,), device_id_type=MESH)
    proj_last.start()

    @pl.when(owner)
    def _():
        wait_bytes(gram_slots.at[pl.ds(0, TILES - 1)], part_send.at[0])
        wait_bytes(gram_slots.at[pl.ds(0, CHIPS - 1)], done_send.at[0])
        wait_bytes(gram_slots.at[pl.ds(0, CHIPS - 1)], done_send.at[0])

    @pl.when(jnp.logical_not(owner))
    def _():
        wait_bytes(gram_slots.at[pl.ds(0, TILES)], part_send.at[0])

    wait_bytes(proj_slots.at[pl.ds(0, CHIPS - 1)], part_send.at[1])
    wait_bytes(proj_slots.at[pl.ds(0, CHIPS - 1)], done_send.at[1])
    gram_last.wait()
    proj_last.wait()


def reduce_all(gram, proj):
    vmem = pl.BlockSpec(memory_space=pltpu.VMEM)
    pair = pltpu.SemaphoreType.DMA((2,))
    return pl.pallas_call(
        reduce_kernel,
        out_shape=(
            jax.ShapeDtypeStruct((2, 256, 256), F32),
            jax.ShapeDtypeStruct((256, 1024), F32),
        ),
        in_specs=[vmem, vmem],
        out_specs=(vmem, vmem),
        scratch_shapes=[
            pltpu.VMEM((128, 256), F32),
            pltpu.VMEM((128, 1024), F32),
            pltpu.VMEM((128, 256), F32),
            pltpu.VMEM((128, 1024), F32),
            pltpu.VMEM((CHIPS, 8, 128), F32),
            pltpu.VMEM((CHIPS, 8, 256), F32),
        ] + [pair] * 8,
        compiler_params=pltpu.CompilerParams(
            collective_id=0, has_side_effects=True, vmem_limit_bytes=32 * 2**20),
        name="reduce_all",
    )(gram, proj)


def near_power(value):
    big = value * F32(2.0**23)
    return (big + value) - big


def grid_slice(value, grid):
    magic = F32(1.5 * 2.0**23 * grid)
    return (value + magic) - magic


def eliminate(block, lane0):
    tiles = [block[8 * t : 8 * t + 8, :] for t in range(PANEL // 8)]
    sub = lax.broadcasted_iota(jnp.int32, (8, 128), 0)
    for k in range(PANEL):
        own, line = divmod(k, 8)
        lane = lane0 + k
        pivot = jnp.broadcast_to(tiles[own][line : line + 1, :], (8, 128))
        inverse = 1.0 / jnp.broadcast_to(pivot[:, lane : lane + 1], (8, 128))
        scaled = pivot * inverse
        for t in range(own, PANEL // 8):
            column = jnp.broadcast_to(tiles[t][:, lane : lane + 1], (8, 128))
            update = column * scaled
            if t == own:
                if line == 7:
                    continue
                update = jnp.where(sub > line, update, 0.0)
            tiles[t] = tiles[t] - update
    return jnp.concatenate(tiles, axis=0)


def factor_kernel(gram_ref, lower_ref, inverse_ref, work, upper):
    n = 256
    high = gram_ref[0]
    row = lax.broadcasted_iota(jnp.int32, (n, n), 0)
    col = lax.broadcasted_iota(jnp.int32, (n, n), 1)
    diagonal = jnp.where(row == col, high, 0.0)
    scale_col = near_power(lax.rsqrt(jnp.sum(diagonal, axis=1, keepdims=True)))
    scale_row = near_power(lax.rsqrt(jnp.sum(diagonal, axis=0, keepdims=True)))
    high = high * scale_col * scale_row
    low = gram_ref[1] * scale_col * scale_row
    eye = jnp.where(row == col, 1.0, 0.0).astype(F32)
    work[:, :n] = high
    work[:, n:] = eye

    lane = lax.broadcasted_iota(jnp.int32, (PANEL, 128), 1)
    line = lax.broadcasted_iota(jnp.int32, (PANEL, 128), 0)
    wide = lax.broadcasted_iota(jnp.int32, (PANEL, n), 1)
    for p in range(n // PANEL):
        first = PANEL * p
        lane0 = first % 128
        tile0 = first - lane0
        here = (lane >= lane0) & (lane < lane0 + PANEL)
        unit = jnp.where(lane == line + (PANEL - lane0), 1.0, 0.0).astype(F32)
        block = jnp.where(here, work[first : first + PANEL, tile0 : tile0 + 128], unit)
        block = eliminate(block, lane0)
        pivots = jnp.sum(jnp.where(lane == line + lane0, block, 0.0), axis=1, keepdims=True)
        block = block * (1.0 / jnp.sqrt(pivots))
        weights = jnp.where(here, 0.0, block)
        rows = work[first : first + PANEL, :]
        zeros = jnp.zeros((PANEL, 2 * n), F32)
        stacked = jnp.concatenate([rows, zeros] if lane0 else [zeros, rows], axis=0)
        solved = mul(weights, stacked)
        left = solved[:, :n]
        left = jnp.where(wide < first + PANEL, 0.0, left)
        right = solved[:, n:]
        if p < n // PANEL - 1:
            step = mul(left, jnp.concatenate([left, right], axis=1), TN)
            work[first + PANEL :, :] = work[first + PANEL :, :] - step[first + PANEL :, :]
        upper[first : first + PANEL, :] = left
        corner = jnp.where(here & (lane >= line + lane0), block, 0.0)
        upper[first : first + PANEL, tile0 : tile0 + 128] = (
            upper[first : first + PANEL, tile0 : tile0 + 128] + corner)
        inverse_ref[first : first + PANEL, :] = right

    lower = upper[...].T
    one = grid_slice(lower, 2.0**-7)
    rest = lower - one
    two = grid_slice(rest, 2.0**-15)
    rest = rest - two
    three = grid_slice(rest, 2.0**-23)
    lower = one + (two + three)
    one, two, three = (s.astype(jnp.bfloat16) for s in (one, two, three))

    def exact(left, right):
        return lax.dot_general(
            jnp.concatenate(left, axis=1), jnp.concatenate(right, axis=1), NT,
            preferred_element_type=F32)

    residual = high - exact([one], [one])
    residual = residual - exact([one, two], [two, one])
    residual = residual - exact([one, two, three], [three, two, one])
    residual = residual - exact([two, three], [three, two])
    residual = residual + low

    first_inverse = inverse_ref[...]
    delta = mul(mul(first_inverse, residual), first_inverse, NT)

    def half(value):
        return jnp.where(row > col, value, jnp.where(row == col, 0.5 * value, 0.0))

    x = half(delta)
    for _ in range(4):
        x = half(delta - mul(x, x, NT))
    square = mul(x, x)
    fourth = mul(square, square)
    total = first_inverse + mul(fourth, first_inverse)
    total = total + mul(square, total)
    total = total - mul(x, total)
    inverse_ref[...] = total * scale_row
    lower_ref[...] = lower * (1.0 / scale_col)


def factor(gram):
    vmem = pl.BlockSpec(memory_space=pltpu.VMEM)
    square = jax.ShapeDtypeStruct((256, 256), F32)
    return pl.pallas_call(
        factor_kernel,
        out_shape=(square, square),
        in_specs=[vmem],
        out_specs=(vmem, vmem),
        scratch_shapes=[pltpu.VMEM((256, 512), F32), pltpu.VMEM((256, 256), F32)],
        compiler_params=pltpu.CompilerParams(vmem_limit_bytes=32 * 2**20),
        name="factor",
    )(gram)


def local(slab, test_matrix):
    total_rows = lax.axis_size("rows") * slab.shape[0]
    root = jnp.sqrt(F32(total_rows))
    sketch, gram, projected = sketch_all(slab, test_matrix)
    gram, projected = reduce_all(gram, projected)
    lower, inverse = factor(gram)
    basis = lax.dot_general(sketch, inverse * root, NT, precision=HIGH)
    coefficients = lax.dot_general(inverse, projected, NN, precision=HIGH)
    return (basis, coefficients, lower / root)


def solution(mesh):
    placed = (P("rows", None), P())
    return jax.shard_map(
        local, mesh=mesh, in_specs=placed, out_specs=(P("rows", None), P(), P()), check_vma=False
    )
```

time: 657 us -> 132 us (0.20)
  waiting for transfers between devices: 420 us -> 0 us
  Pallas kernels: 0 us -> 119 us
  other arithmetic: 112 us -> 0.72 us
  matrix products: 74.7 us -> 10.9 us
  local copies, waits for them, and re-layouts: 29.5 us -> 1.03 us
  between operations: 17.1 us -> 0.66 us
    psum x3 -> x0, waiting for transfers between devices: 420 us -> none  [the longest x1 145 us: local(): gram = lax.psum(row_gram(sketch), 'rows')]
    pallas_call x0 -> x3, Pallas kernels: none -> 119 us  [the longest x1 42.9 us: reduce_all(): pl.pallas_call(reduce_kernel, out_shape=(jax.ShapeDtypeStruct((2, 256, 25...]
    another operation x17 -> x0, other arithmetic: 108 us -> none  [the longest x13 68.7 us: factor_pair(): lower = jnp.linalg.cholesky(gram)]
    dot_general x6 -> x2, matrix products: 72 us -> 10.9 us  [the longest x1 8.95 us: local(): basis = lax.dot_general(sketch, inverse * root, NT, precision=HIGH)]
    unnamed x10 -> x2, local copies, waits for them, and re-layouts: 19.2 us -> 1.03 us
    another operation x19 -> x0, local copies, waits for them, and re-layouts: 8.22 us -> none  [the longest x15 8.17 us: factor_pair(): lax.linalg.triangular_solve(lower, eye, left_side=True, lower=True)]
  transfers between devices with their start and end apart: 3 -> 0, of which waited for: 3 -> 0; matrix products, arithmetic and copies ran while one was open for 1% -> 0% of each run, Pallas kernels for 0% -> 0%
where the time goes in v1:
time: 132 us
  Pallas kernels  119 us (90%)
  matrix products  10.9 us (8%)
    pallas_call x1, Pallas kernels, reduce_all(): pl.pallas_call(reduce_kernel, out_shape=(jax.ShapeDtypeStruct((2, 256, 25...  42.9 us
    pallas_call x1, Pallas kernels, factor(): pl.pallas_call(factor_kernel, out_shape=(square, square), in_specs=[vmem]...  42.4 us
    pallas_call x1, Pallas kernels, sketch_all(): pl.pallas_call(sketch_kernel, grid=(rows // CHUNK,), out_shape=(jax.Shape...  33.2 us
    dot_general x1, matrix products, local(): basis = lax.dot_general(sketch, inverse * root, NT, precision=HIGH)  8.95 us

profile of v1, /device:TPU:1, one launch (start us, length us, event | category | flops | bytes accessed | tf_op | source)
XLA Modules:
  0.0 131.9 jit_solution(15677162969822310578)
XLA Ops:
  0.6 0.0 copy-start
  0.6 1.0 copy-done
  1.7 33.2 %sketch_all.1 = (f32[8192,256]{1,0:T(8,128)S(1)}, f32[256,256]{1,0:T(8,128)S(1)}, f32[256,1024]{1,0:T(8,128)S(1)}) custom-call(bf16[8192,1024]{1,0:T(8,128)(2,1)} %slab_ref.1, bf16[1024,256]{1,0:T(8,128)(2,1)S(1)} %copy-done), custom_call_target="tpu_custom_call" | custom-call | tf_op jit(solution)/shard_map/sketch_all/pallas_call | solution.py:76
  34.9 42.9 %reduce_all.1 = (f32[2,256,256]{2,1,0:T(8,128)S(1)}, f32[256,1024]{1,0:T(8,128)S(1)}) custom-call(f32[256,256]{1,0:T(8,128)S(1)} %get-tuple-element.11.gram_ref, f32[256,1024]{1,0:T(8,128)S(1)} %get-tuple-element.12.proj_ref), custom_call_target="tpu_custom_call" | custom-call | tf_op jit(solution)/shard_map/reduce_all/pallas_call | solution.py:265
  77.8 42.4 %factor.1 = (f32[256,256]{1,0:T(8,128)S(1)}, f32[256,256]{1,0:T(8,128)S(1)}) custom-call(f32[2,256,256]{2,1,0:T(8,128)S(1)} %get-tuple-element.13.gram_ref), custom_call_target="tpu_custom_call" | custom-call | tf_op jit(solution)/shard_map/factor/pallas_call | solution.py:402
  120.3 0.7 broadcast_multiply_fusion
  121.0 2.0 %fusion.4 = f32[256,1024]{1,0:T(8,128)} fusion(f32[256,256]{1,0:T(8,128)S(1)} %get-tuple-element.14, f32[256,1024]{1,0:T(8,128)S(1)} %get-tuple-element.15), kind=kOutput, calls=%fused_computation.5 | convolution fusion | flops 805306368 | bytes 2359296 | tf_op jit(solution)/shard_map/dot_general | solution.py:420
  123.0 8.9 %fusion = f32[8192,256]{1,0:T(8,128)} fusion(f32[8192,256]{1,0:T(8,128)S(1)} %get-tuple-element.10, f32[256,256]{1,0:T(8,128)S(1)} %get-tuple-element.14), kind=kOutput, calls=%fused_computation | convolution fusion | flops 6442516480 | bytes 17039360 | tf_op jit(solution)/shard_map/dot_general | solution.py:419
Async XLA Ops:
  0.6 1.0 copy-start

commit v2 on v0

v2 whole, which is shorter than its diff:
```python
import functools

import jax
import jax.numpy as jnp
from jax import lax
from jax.experimental import pallas as pl
from jax.experimental.pallas import tpu as pltpu
from jax.sharding import PartitionSpec as P

F32 = jnp.float32
HIGH = lax.Precision.HIGHEST
MESH = pl.DeviceIdType.MESH
NN = (((1,), (0,)), ((), ()))
NT = (((1,), (1,)), ((), ()))
TN = (((0,), (0,)), ((), ()))
PANEL = 64


def mul(left, right, dims=NN):
    return lax.dot_general(left, right, dims, precision=HIGH, preferred_element_type=F32)


def split(value):
    upper = value.astype(jnp.bfloat16)
    return upper, (value - upper.astype(F32)).astype(jnp.bfloat16)


def mul3(left, right, dims=NN):
    a, b = split(left)
    c, d = split(right)

    def one(x, y):
        return lax.dot_general(x, y, dims, preferred_element_type=F32)

    return one(a, c) + (one(a, d) + one(b, c))


def two_sum(a, b):
    total = a + b
    part = total - a
    return total, (a - (total - part)) + (b - part)


class Place:
    def __init__(self):
        me = lax.axis_index("rows")
        self.x = me // 32
        self.member = (me // 2) % 16
        self.core = me % 2

    def mate(self):
        return self.x * 32 + self.member * 2 + 1 - self.core

    def in_plane(self, step):
        member = (self.member + step) % 16
        return member, self.x * 32 + member * 2 + self.core

    def along_x(self, step):
        x = (self.x + step) % 4
        return x * 32 + self.member * 2 + self.core

    def signal(self):
        barrier = pltpu.get_barrier_semaphore()

        def signal(device):
            pl.semaphore_signal(barrier, inc=1, device_id=(device,), device_id_type=MESH)

        def plane(step, carry):
            signal(self.in_plane(step)[1])
            return carry

        signal(self.mate())
        lax.fori_loop(1, 16, plane, 0)
        for step in range(1, 4):
            signal(self.along_x(step))

    def wait(self):
        pl.semaphore_wait(pltpu.get_barrier_semaphore(), 19)


def eight(index):
    return pl.ds(pl.multiple_of(index * 8, 8), 8)


def half_rows(core):
    return pl.ds(pl.multiple_of(core * 128, 128), 128)


def wait_bytes(ref, sem):
    pltpu.make_async_copy(ref, ref, sem).wait()


class Reduction:
    def __init__(self, place, source, out, pair, half, plane, strip, line, send, recv, exact):
        self.place, self.source, self.out, self.pair, self.half = place, source, out, pair, half
        self.plane, self.strip, self.line = plane, strip, line
        self.send, self.recv, self.exact = send, recv, exact

    def copy(self, phase, src, dst, device):
        return pltpu.make_async_remote_copy(
            src_ref=src, dst_ref=dst, send_sem=self.send.at[phase], recv_sem=self.recv.at[phase],
            device_id=(device,), device_id_type=MESH)

    def swap(self):
        place = self.place
        return self.copy(0, self.source.at[half_rows(1 - place.core)], self.pair, place.mate())

    def start_swap(self):
        self.swap().start()

    def to_plane(self):
        place = self.place
        self.swap().wait_recv()
        self.half[...] = self.source[half_rows(place.core), :] + self.pair[...]
        self.plane[place.member] = self.half[eight(place.member), :]

        def send(step, carry):
            member, device = place.in_plane(step)
            self.copy(1, self.half.at[eight(member)], self.plane.at[place.member], device).start()
            return carry

        lax.fori_loop(1, 16, send, 0)

    def add(self, terms):
        if not self.exact:
            total = terms[0][0]
            for term in terms[1:]:
                total = total + term[0]
            return (total,)
        high, low = terms[0][0], jnp.zeros_like(terms[0][0])
        for term in terms[1:]:
            high, error = two_sum(high, term[0])
            low = low + error
        for term in terms:
            if len(term) > 1:
                low = low + term[1]
        high, low = two_sum(high, low)
        return high, low

    def to_line(self):
        place = self.place
        wait_bytes(self.plane.at[pl.ds(0, 15)], self.recv.at[1])
        for index, value in enumerate(self.add([(self.plane[t],) for t in range(16)])):
            self.strip[index] = value
            self.line[place.x, index] = value
        for step in range(1, 4):
            self.copy(2, self.strip, self.line.at[place.x], place.along_x(step)).start()

    def back_to_plane(self):
        place = self.place
        wait_bytes(self.line.at[pl.ds(0, 3)], self.recv.at[2])
        planes = self.strip.shape[0]
        rows = eight(place.core * 16 + place.member)
        terms = [[self.line[x, index] for index in range(planes)] for x in range(4)]
        for index, value in enumerate(self.add(terms)):
            self.out[index, rows, :] = value

        def send(step, carry):
            self.copy(3, self.out.at[:, rows], self.out.at[:, rows], place.in_plane(step)[1]).start()
            return carry

        lax.fori_loop(1, 16, send, 0)

    def last(self):
        place = self.place
        rows = half_rows(place.core)
        return self.copy(4, self.out.at[:, rows], self.out.at[:, rows], place.mate())

    def back_to_mate(self):
        wait_bytes(self.out.at[:, pl.ds(0, 120)], self.recv.at[3])
        self.last().start()

    def finish(self):
        self.last().wait_recv()

    def drain(self):
        self.swap().wait_send()
        wait_bytes(self.plane.at[pl.ds(0, 15)], self.send.at[1])
        wait_bytes(self.line.at[pl.ds(0, 3)], self.send.at[2])
        wait_bytes(self.out.at[:, pl.ds(0, 120)], self.send.at[3])
        self.last().wait_send()


def reduction_scratch(width, planes):
    return [
        pltpu.VMEM((128, width), F32),
        pltpu.VMEM((128, width), F32),
        pltpu.VMEM((16, 8, width), F32),
        pltpu.VMEM((planes, 8, width), F32),
        pltpu.VMEM((4, planes, 8, width), F32),
        pltpu.SemaphoreType.DMA((5,)),
        pltpu.SemaphoreType.DMA((5,)),
    ]


def near_power(value):
    big = value * F32(2.0**23)
    return (big + value) - big


def grid_slice(value, grid):
    magic = F32(1.5 * 2.0**23 * grid)
    return (value + magic) - magic


def reciprocal(value):
    guess = pl.reciprocal(value, approx=True)
    guess = guess * (2.0 - value * guess)
    return guess * (2.0 - value * guess)


def eliminate(block, lane0):
    count = PANEL // 8
    tiles = [block[8 * t : 8 * t + 8, :] for t in range(count)]
    sub = lax.broadcasted_iota(jnp.int32, (8, 128), 0)

    def spread(value, lane):
        return jnp.broadcast_to(value[:, lane : lane + 1], (8, 128))

    for own in range(count):
        lane = lane0 + 8 * own
        pivots = [jnp.broadcast_to(tiles[own][j : j + 1, :], (8, 128)) for j in range(8)]
        columns = {
            t: [spread(tiles[t], lane + j) for j in range(8)] for t in range(own + 1, count)}
        head = [[spread(pivots[i], lane + j) if j >= i else None for j in range(8)] for i in range(8)]
        scaled = []
        ratio = [[None] * 8 for _ in range(8)]
        for i in range(8):
            inverse = reciprocal(head[i][i])
            for j in range(i + 1, 8):
                ratio[i][j] = head[i][j] * inverse
                for q in range(j, 8):
                    head[j][q] = head[j][q] - ratio[i][j] * head[i][q]
                pivots[j] = pivots[j] - ratio[i][j] * pivots[i]
            scaled.append(pivots[i] * inverse)
        for t in range(own + 1, count):
            done = []
            for j in range(8):
                column = columns[t][j]
                for i in range(j):
                    column = column - done[i] * ratio[i][j]
                done.append(column)
                tiles[t] = tiles[t] - column * scaled[j]
        result = pivots[0]
        for j in range(1, 8):
            result = jnp.where(sub == j, pivots[j], result)
        tiles[own] = result
    return jnp.concatenate(tiles, axis=0)


def factor_gram(gram_ref, lower_ref, inverse_ref, work, upper, between):
    n = 256
    high = gram_ref[0]
    row = lax.broadcasted_iota(jnp.int32, (n, n), 0)
    col = lax.broadcasted_iota(jnp.int32, (n, n), 1)
    diagonal = jnp.where(row == col, high, 0.0)
    scale_col = near_power(lax.rsqrt(jnp.sum(diagonal, axis=1, keepdims=True)))
    scale_row = near_power(lax.rsqrt(jnp.sum(diagonal, axis=0, keepdims=True)))
    high = high * scale_col * scale_row
    low = gram_ref[1] * scale_col * scale_row
    eye = jnp.where(row == col, 1.0, 0.0).astype(F32)
    work[:, :n] = high
    work[:, n:] = eye

    lane = lax.broadcasted_iota(jnp.int32, (PANEL, 128), 1)
    line = lax.broadcasted_iota(jnp.int32, (PANEL, 128), 0)
    wide = lax.broadcasted_iota(jnp.int32, (PANEL, n), 1)
    for p in range(n // PANEL):
        first = PANEL * p
        lane0 = first % 128
        tile0 = first - lane0
        here = (lane >= lane0) & (lane < lane0 + PANEL)
        unit = jnp.where(lane == line + (PANEL - lane0), 1.0, 0.0).astype(F32)
        block = jnp.where(here, work[first : first + PANEL, tile0 : tile0 + 128], unit)
        block = eliminate(block, lane0)
        pivots = jnp.sum(jnp.where(lane == line + lane0, block, 0.0), axis=1, keepdims=True)
        block = block * (1.0 / jnp.sqrt(pivots))
        weights = jnp.where(here, 0.0, block)
        rows = work[first : first + PANEL, :]
        zeros = jnp.zeros((PANEL, 2 * n), F32)
        stacked = jnp.concatenate([rows, zeros] if lane0 else [zeros, rows], axis=0)
        solved = mul(weights, stacked)
        left = solved[:, :n]
        left = jnp.where(wide < first + PANEL, 0.0, left)
        right = solved[:, n:]
        if p < n // PANEL - 1:
            step = mul(left, jnp.concatenate([left, right], axis=1), TN)
            work[first + PANEL :, :] = work[first + PANEL :, :] - step[first + PANEL :, :]
        upper[first : first + PANEL, :] = left
        corner = jnp.where(here & (lane >= line + lane0), block, 0.0)
        upper[first : first + PANEL, tile0 : tile0 + 128] = (
            upper[first : first + PANEL, tile0 : tile0 + 128] + corner)
        inverse_ref[first : first + PANEL, :] = right
        between(p)

    lower = upper[...].T
    one = grid_slice(lower, 2.0**-7)
    rest = lower - one
    two = grid_slice(rest, 2.0**-15)
    rest = rest - two
    three = grid_slice(rest, 2.0**-23)
    lower = one + (two + three)
    one, two, three = (s.astype(jnp.bfloat16) for s in (one, two, three))

    def exact(left, right):
        return lax.dot_general(
            jnp.concatenate(left, axis=1), jnp.concatenate(right, axis=1), NT,
            preferred_element_type=F32)

    residual = high - exact([one], [one])
    residual = residual - exact([one, two], [two, one])
    residual = residual - exact([one, two, three], [three, two, one])
    residual = residual - exact([two, three], [three, two])
    residual = residual + low

    first_inverse = inverse_ref[...]
    delta = mul3(mul3(first_inverse, residual), first_inverse, NT)

    def half(value):
        return jnp.where(row > col, value, jnp.where(row == col, 0.5 * value, 0.0))

    x = half(delta)
    for _ in range(3):
        x = half(delta - mul3(x, x, NT))
    square = mul3(x, x)
    fourth = mul3(square, square)
    total = first_inverse + mul3(fourth, first_inverse)
    total = total + mul3(square, total)
    total = total - mul3(x, total)
    inverse_ref[...] = total * scale_row
    lower_ref[...] = lower * (1.0 / scale_col)


CHUNK = 1024
CHUNKS = 8
GROUPS = (1, 2, 2, 3)


def main_kernel(
    slab_hbm, test_ref, sketch_hbm, lower_ref, inverse_ref, proj_out,
    slab, sketch, turned, gram, low, cross, proj, gram_out, work, upper, load_sem, store_sem,
    *scratch,
):
    place = Place()
    gram_sum = Reduction(place, gram, gram_out, *scratch[:7], exact=True)
    proj_sum = Reduction(place, proj, proj_out, *scratch[7:], exact=False)

    def rows_of(index):
        return pl.ds(index * CHUNK, CHUNK)

    def load(index):
        rows = rows_of(index)
        return pltpu.make_async_copy(slab_hbm.at[rows], slab.at[rows], load_sem.at[index])

    def store(index):
        rows = rows_of(index)
        return pltpu.make_async_copy(sketch.at[rows], sketch_hbm.at[rows], store_sem.at[index])

    for index in range(CHUNKS):
        load(index).start()
    place.signal()
    gram[...] = jnp.zeros_like(gram)
    low[...] = jnp.zeros_like(low)
    cross[...] = jnp.zeros_like(cross)
    proj[...] = jnp.zeros_like(proj)

    def make_sketch(index):
        rows = rows_of(index)
        value = jnp.dot(slab[rows, :], test_ref[...], preferred_element_type=F32)
        sketch[rows, :] = value
        turned[:, rows] = value.T

    def outer(left, right):
        return lax.dot_general(left, right, NT, preferred_element_type=F32)

    def add_gram(index):
        value = turned[:, rows_of(index)]
        most = jnp.max(jnp.abs(value), axis=1, keepdims=True)
        magic = near_power(1.5 * most) * F32(1.5 * 2.0**16)
        one = (value + magic) - magic
        rest = value - one
        two, three = split(rest)
        one = one.astype(jnp.bfloat16)
        total, error = two_sum(gram[...], outer(one, one))
        gram[...] = total
        low[...] += error + outer(two, two)
        cross[...] += outer(one, two) + outer(one, three)

    def add_proj(index):
        rows = rows_of(index)
        block = slab[rows, :]
        one, two = split(turned[:, rows])
        proj[...] += jnp.dot(one, block, preferred_element_type=F32) + jnp.dot(
            two, block, preferred_element_type=F32)

    done = 0
    for count in GROUPS:
        for index in range(done, done + count):
            load(index).wait()
        for index in range(done, done + count):
            make_sketch(index)
            if index:
                add_gram(index - 1)
        done += count
    add_gram(CHUNKS - 1)
    mixed = cross[...]
    gram[...] += (mixed + mixed.T) + low[...]

    place.wait()
    gram_sum.start_swap()
    for index in range(CHUNKS):
        store(index).start()
    add_proj(0)
    add_proj(1)
    gram_sum.to_plane()
    add_proj(2)
    add_proj(3)
    gram_sum.to_line()
    add_proj(4)
    add_proj(5)
    gram_sum.back_to_plane()
    add_proj(6)
    add_proj(7)
    gram_sum.back_to_mate()
    proj_sum.start_swap()
    gram_sum.finish()

    steps = (proj_sum.to_plane, proj_sum.to_line, proj_sum.back_to_plane, proj_sum.back_to_mate)
    factor_gram(gram_out, lower_ref, inverse_ref, work, upper, lambda panel: steps[panel]())
    proj_sum.finish()
    gram_sum.drain()
    proj_sum.drain()
    for index in range(CHUNKS):
        store(index).wait()


def reduced_factors(slab, test_matrix):
    rows = slab.shape[0]
    vmem = pl.BlockSpec(memory_space=pltpu.VMEM)
    anywhere = pl.BlockSpec(memory_space=pl.ANY)
    square = jax.ShapeDtypeStruct((256, 256), F32)
    return pl.pallas_call(
        main_kernel,
        out_shape=(
            jax.ShapeDtypeStruct((rows, 256), F32),
            square,
            square,
            jax.ShapeDtypeStruct((1, 256, 1024), F32),
        ),
        in_specs=[anywhere, vmem],
        out_specs=(anywhere, vmem, vmem, vmem),
        scratch_shapes=[
            pltpu.VMEM((rows, 1024), jnp.bfloat16),
            pltpu.VMEM((rows, 256), F32),
            pltpu.VMEM((256, rows), F32),
            pltpu.VMEM((256, 256), F32),
            pltpu.VMEM((256, 256), F32),
            pltpu.VMEM((256, 256), F32),
            pltpu.VMEM((256, 1024), F32),
            pltpu.VMEM((2, 256, 256), F32),
            pltpu.VMEM((256, 512), F32),
            pltpu.VMEM((256, 256), F32),
            pltpu.SemaphoreType.DMA((CHUNKS,)),
            pltpu.SemaphoreType.DMA((CHUNKS,)),
        ] + reduction_scratch(256, 2) + reduction_scratch(1024, 1),
        compiler_params=pltpu.CompilerParams(
            collective_id=0, has_side_effects=True, vmem_limit_bytes=60 * 2**20),
        name="reduced_factors",
    )(slab, test_matrix)


def basis_kernel(root, sketch_ref, lower_ref, inverse_ref, proj_ref, basis_ref, coef_ref, factor_ref):
    @pl.when(pl.program_id(0) == 0)
    def _():
        coef_ref[...] = mul(inverse_ref[...], proj_ref[0])
        factor_ref[...] = lower_ref[...] * F32(1.0 / root)

    basis_ref[...] = mul(sketch_ref[...], inverse_ref[...] * F32(root), NT)


def outputs(sketch, lower, inverse, proj, root):
    rows = sketch.shape[0]
    square = pl.BlockSpec((256, 256), lambda i: (0, 0))
    return pl.pallas_call(
        functools.partial(basis_kernel, root),
        grid=(rows // CHUNK,),
        out_shape=(
            jax.ShapeDtypeStruct((rows, 256), F32),
            jax.ShapeDtypeStruct((256, 1024), F32),
            jax.ShapeDtypeStruct((256, 256), F32),
        ),
        in_specs=[
            pl.BlockSpec((CHUNK, 256), lambda i: (i, 0)),
            square,
            square,
            pl.BlockSpec((1, 256, 1024), lambda i: (0, 0, 0)),
        ],
        out_specs=(
            pl.BlockSpec((CHUNK, 256), lambda i: (i, 0)),
            pl.BlockSpec((256, 1024), lambda i: (0, 0)),
            square,
        ),
        compiler_params=pltpu.CompilerParams(vmem_limit_bytes=60 * 2**20),
        name="outputs",
    )(sketch, lower, inverse, proj)


def local(slab, test_matrix):
    root = float((lax.axis_size("rows") * slab.shape[0]) ** 0.5)
    sketch, lower, inverse, proj = reduced_factors(slab, test_matrix)
    return outputs(sketch, lower, inverse, proj, root)


def solution(mesh):
    placed = (P("rows", None), P())
    return jax.shard_map(
        local, mesh=mesh, in_specs=placed, out_specs=(P("rows", None), P(), P()), check_vma=False
    )
```

time: 657 us -> 83.1 us (0.13)
  waiting for transfers between devices: 420 us -> 0 us
  other arithmetic: 112 us -> 0 us
  Pallas kernels: 0 us -> 82.1 us
  matrix products: 74.7 us -> 0 us
  local copies, waits for them, and re-layouts: 29.5 us -> 0 us
  between operations: 17.1 us -> 0.64 us
    psum x3 -> x0, waiting for transfers between devices: 420 us -> none  [the longest x1 145 us: local(): gram = lax.psum(row_gram(sketch), 'rows')]
    another operation x17 -> x0, other arithmetic: 108 us -> none  [the longest x13 68.7 us: factor_pair(): lower = jnp.linalg.cholesky(gram)]
    pallas_call x0 -> x2, Pallas kernels: none -> 82.1 us  [the longest x1 68.1 us: reduced_factors(): pl.pallas_call(main_kernel, out_shape=(jax.ShapeDtypeStruct((rows, 256),...]
    dot_general x6 -> x0, matrix products: 72 us -> none  [the longest x2 29 us: row_gram(): lax.dot_general(left, left, (((0,), (0,)), ((), ())), precision=lax.Preci...]
    unnamed x10 -> x0, local copies, waits for them, and re-layouts: 19.2 us -> none
    another operation x19 -> x0, local copies, waits for them, and re-layouts: 8.22 us -> none  [the longest x15 8.17 us: factor_pair(): lax.linalg.triangular_solve(lower, eye, left_side=True, lower=True)]
  transfers between devices with their start and end apart: 3 -> 0, of which waited for: 3 -> 0; matrix products, arithmetic and copies ran while one was open for 1% -> 0% of each run, Pallas kernels for 0% -> 0%
where the time goes in v2:
time: 83.1 us; the launch traced here: 82.7 us
  Pallas kernels  82.1 us (99%)
    pallas_call x1, Pallas kernels, reduced_factors(): pl.pallas_call(main_kernel, out_shape=(jax.ShapeDtypeStruct((rows, 256),...  68.1 us
    pallas_call x1, Pallas kernels, outputs(): pl.pallas_call(functools.partial(basis_kernel, root), grid=(rows // CHUNK...  14 us

profile of v2, /device:TPU:1, one launch (start us, length us, event | category | flops | bytes accessed | tf_op | source)
XLA Modules:
  0.0 82.7 jit_solution(6090577719454093380)
XLA Ops:
  0.6 68.1 %reduced_factors.1 = (f32[8192,256]{1,0:T(8,128)}, f32[256,256]{1,0:T(8,128)}, f32[256,256]{1,0:T(8,128)}, f32[1,256,1024]{2,1,0:T(8,128)}) custom-call(bf16[8192,1024]{1,0:T(8,128)(2,1)} %slab_hbm.1, bf16[1024,256]{1,0:T(8,128)(2,1)} %test_ref.1), custom_call_target="tpu_custom_call" | custom-call | tf_op jit(solution)/shard_map/reduced_factors/pallas_call | solution.py:442
  68.8 14.0 %outputs.1 = (f32[8192,256]{1,0:T(8,128)}, f32[256,1024]{1,0:T(8,128)}, f32[256,256]{1,0:T(8,128)}) custom-call(f32[8192,256]{1,0:T(8,128)} %get-tuple-element.7.sketch_ref, f32[256,256]{1,0:T(8,128)} %get-tuple-element.8.lower_ref, f32[256,256]{1,0:T(8,128)} %get-tuple-element.9.inverse_ref, f32[1,256,1024]{2,1,0:T(8,128)} %get-tuple-element.10.proj_ref), custom_call_target="tpu_custom_call" | custom-call | tf_op jit(solution)/shard_map/outputs/pallas_call | solution.py:484

commit v3 on v2

--- a/solution.py
+++ b/solution.py
@@ -209,7 +209,7 @@
     return guess * (2.0 - value * guess)
 
 
-def eliminate(block, lane0):
+def eliminate(block):
     count = PANEL // 8
     tiles = [block[8 * t : 8 * t + 8, :] for t in range(count)]
     sub = lax.broadcasted_iota(jnp.int32, (8, 128), 0)
@@ -218,7 +218,7 @@
         return jnp.broadcast_to(value[:, lane : lane + 1], (8, 128))
 
     for own in range(count):
-        lane = lane0 + 8 * own
+        lane = 8 * own
         pivots = [jnp.broadcast_to(tiles[own][j : j + 1, :], (8, 128)) for j in range(8)]
         columns = {
             t: [spread(tiles[t], lane + j) for j in range(8)] for t in range(own + 1, count)}
@@ -265,33 +265,33 @@
     lane = lax.broadcasted_iota(jnp.int32, (PANEL, 128), 1)
     line = lax.broadcasted_iota(jnp.int32, (PANEL, 128), 0)
     wide = lax.broadcasted_iota(jnp.int32, (PANEL, n), 1)
-    for p in range(n // PANEL):
-        first = PANEL * p
-        lane0 = first % 128
-        tile0 = first - lane0
-        here = (lane >= lane0) & (lane < lane0 + PANEL)
-        unit = jnp.where(lane == line + (PANEL - lane0), 1.0, 0.0).astype(F32)
-        block = jnp.where(here, work[first : first + PANEL, tile0 : tile0 + 128], unit)
-        block = eliminate(block, lane0)
-        pivots = jnp.sum(jnp.where(lane == line + lane0, block, 0.0), axis=1, keepdims=True)
+    front = lane < PANEL
+    unit = jnp.where(lane == line + PANEL, 1.0, 0.0).astype(F32)
+
+    def panel_step(p, carry):
+        rows = pl.ds(pl.multiple_of(PANEL * p, PANEL), PANEL)
+        tile = pl.ds(pl.multiple_of((p // 2) * 128, 128), 128)
+        odd = jnp.broadcast_to(p % 2, (PANEL, 128)) == 1
+
+        def turn(value):
+            return jnp.where(odd, pltpu.roll(value, PANEL, 1), value)
+
+        block = eliminate(jnp.where(front, turn(work[rows, tile]), unit))
+        pivots = jnp.sum(jnp.where(lane == line, block, 0.0), axis=1, keepdims=True)
         block = block * (1.0 / jnp.sqrt(pivots))
-        weights = jnp.where(here, 0.0, block)
-        rows = work[first : first + PANEL, :]
-        zeros = jnp.zeros((PANEL, 2 * n), F32)
-        stacked = jnp.concatenate([rows, zeros] if lane0 else [zeros, rows], axis=0)
+        weights = jnp.where(front, 0.0, block)
+        stacked = jnp.concatenate([jnp.zeros((PANEL, 2 * n), F32), work[rows, :]], axis=0)
         solved = mul(weights, stacked)
-        left = solved[:, :n]
-        left = jnp.where(wide < first + PANEL, 0.0, left)
+        left = jnp.where(wide < PANEL * (p + 1), 0.0, solved[:, :n])
         right = solved[:, n:]
-        if p < n // PANEL - 1:
-            step = mul(left, jnp.concatenate([left, right], axis=1), TN)
-            work[first + PANEL :, :] = work[first + PANEL :, :] - step[first + PANEL :, :]
-        upper[first : first + PANEL, :] = left
-        corner = jnp.where(here & (lane >= line + lane0), block, 0.0)
-        upper[first : first + PANEL, tile0 : tile0 + 128] = (
-            upper[first : first + PANEL, tile0 : tile0 + 128] + corner)
-        inverse_ref[first : first + PANEL, :] = right
+        work[...] = work[...] - mul(left, jnp.concatenate([left, right], axis=1), TN)
+        upper[rows, :] = left
+        upper[rows, tile] = upper[rows, tile] + turn(jnp.where(front & (lane >= line), block, 0.0))
+        inverse_ref[rows, :] = right
         between(p)
+        return carry
+
+    lax.fori_loop(0, n // PANEL, panel_step, 0)
 
     lower = upper[...].T
     one = grid_slice(lower, 2.0**-7)
@@ -320,8 +320,7 @@
         return jnp.where(row > col, value, jnp.where(row == col, 0.5 * value, 0.0))
 
     x = half(delta)
-    for _ in range(3):
-        x = half(delta - mul3(x, x, NT))
+    x = lax.fori_loop(0, 3, lambda _, x: half(delta - mul3(x, x, NT)), x)
     square = mul3(x, x)
     fourth = mul3(square, square)
     total = first_inverse + mul3(fourth, first_inverse)
@@ -337,13 +336,14 @@
 
 
 def main_kernel(
-    slab_hbm, test_ref, sketch_hbm, lower_ref, inverse_ref, proj_out,
-    slab, sketch, turned, gram, low, cross, proj, gram_out, work, upper, load_sem, store_sem,
+    slab_hbm, test_ref, sketch, lower_ref, inverse_ref, left_out, right_out,
+    slab, turned, gram, low, cross, left, right, gram_out, work, upper, load_sem,
     *scratch,
 ):
     place = Place()
     gram_sum = Reduction(place, gram, gram_out, *scratch[:7], exact=True)
-    proj_sum = Reduction(place, proj, proj_out, *scratch[7:], exact=False)
+    left_sum = Reduction(place, left, left_out, *scratch[7:14], exact=False)
+    right_sum = Reduction(place, right, right_out, *scratch[14:], exact=False)
 
     def rows_of(index):
         return pl.ds(index * CHUNK, CHUNK)
@@ -351,10 +351,6 @@
     def load(index):
         rows = rows_of(index)
         return pltpu.make_async_copy(slab_hbm.at[rows], slab.at[rows], load_sem.at[index])
-
-    def store(index):
-        rows = rows_of(index)
-        return pltpu.make_async_copy(sketch.at[rows], sketch_hbm.at[rows], store_sem.at[index])
 
     for index in range(CHUNKS):
         load(index).start()
@@ -362,7 +358,6 @@
     gram[...] = jnp.zeros_like(gram)
     low[...] = jnp.zeros_like(low)
     cross[...] = jnp.zeros_like(cross)
-    proj[...] = jnp.zeros_like(proj)
 
     def make_sketch(index):
         rows = rows_of(index)
@@ -386,12 +381,22 @@
         low[...] += error + outer(two, two)
         cross[...] += outer(one, two) + outer(one, three)
 
-    def add_proj(index):
-        rows = rows_of(index)
-        block = slab[rows, :]
-        one, two = split(turned[:, rows])
-        proj[...] += jnp.dot(one, block, preferred_element_type=F32) + jnp.dot(
-            two, block, preferred_element_type=F32)
+    def project(part):
+        side, quarter = divmod(part, 4)
+        target = (left, right)[side]
+        if quarter == 0:
+            target[...] = jnp.zeros_like(target)
+
+        def add(index, carry):
+            rows = pl.ds(pl.multiple_of(index * CHUNK, CHUNK), CHUNK)
+            block = slab[rows, side * 512 : side * 512 + 512]
+            one, two = split(turned[:, rows])
+            term = jnp.dot(one, block, preferred_element_type=F32) + jnp.dot(
+                two, block, preferred_element_type=F32)
+            target[...] += term
+            return carry
+
+        lax.fori_loop(2 * quarter, 2 * quarter + 2, add, 0)
 
     done = 0
     for count in GROUPS:
@@ -408,30 +413,49 @@
 
     place.wait()
     gram_sum.start_swap()
-    for index in range(CHUNKS):
-        store(index).start()
-    add_proj(0)
-    add_proj(1)
+    project(0)
     gram_sum.to_plane()
-    add_proj(2)
-    add_proj(3)
+    project(1)
+    project(2)
     gram_sum.to_line()
-    add_proj(4)
-    add_proj(5)
+    project(3)
+    left_sum.start_swap()
+    project(4)
     gram_sum.back_to_plane()
-    add_proj(6)
-    add_proj(7)
+    project(5)
+    left_sum.to_plane()
+    project(6)
     gram_sum.back_to_mate()
-    proj_sum.start_swap()
+    project(7)
+    right_sum.start_swap()
+    left_sum.to_line()
     gram_sum.finish()
 
-    steps = (proj_sum.to_plane, proj_sum.to_line, proj_sum.back_to_plane, proj_sum.back_to_mate)
-    factor_gram(gram_out, lower_ref, inverse_ref, work, upper, lambda panel: steps[panel]())
-    proj_sum.finish()
+    def between(panel):
+        @pl.when(panel == 0)
+        def _():
+            right_sum.to_plane()
+            left_sum.back_to_plane()
+
+        @pl.when(panel == 1)
+        def _():
+            right_sum.to_line()
+            left_sum.back_to_mate()
+
+        @pl.when(panel == 2)
+        def _():
+            right_sum.back_to_plane()
+
+        @pl.when(panel == 3)
+        def _():
+            right_sum.back_to_mate()
+
+    factor_gram(gram_out, lower_ref, inverse_ref, work, upper, between)
+    left_sum.finish()
+    right_sum.finish()
     gram_sum.drain()
-    proj_sum.drain()
-    for index in range(CHUNKS):
-        store(index).wait()
+    left_sum.drain()
+    right_sum.drain()
 
 
 def reduced_factors(slab, test_matrix):
@@ -445,70 +469,70 @@
             jax.ShapeDtypeStruct((rows, 256), F32),
             square,
             square,
-            jax.ShapeDtypeStruct((1, 256, 1024), F32),
+            jax.ShapeDtypeStruct((1, 256, 512), F32),
+            jax.ShapeDtypeStruct((1, 256, 512), F32),
         ),
         in_specs=[anywhere, vmem],
-        out_specs=(anywhere, vmem, vmem, vmem),
+        out_specs=(vmem,) * 5,
         scratch_shapes=[
             pltpu.VMEM((rows, 1024), jnp.bfloat16),
-            pltpu.VMEM((rows, 256), F32),
             pltpu.VMEM((256, rows), F32),
             pltpu.VMEM((256, 256), F32),
             pltpu.VMEM((256, 256), F32),
             pltpu.VMEM((256, 256), F32),
-            pltpu.VMEM((256, 1024), F32),
+            pltpu.VMEM((256, 512), F32),
+            pltpu.VMEM((256, 512), F32),
             pltpu.VMEM((2, 256, 256), F32),
             pltpu.VMEM((256, 512), F32),
             pltpu.VMEM((256, 256), F32),
             pltpu.SemaphoreType.DMA((CHUNKS,)),
-            pltpu.SemaphoreType.DMA((CHUNKS,)),
-        ] + reduction_scratch(256, 2) + reduction_scratch(1024, 1),
+        ] + reduction_scratch(256, 2) + reduction_scratch(512, 1) * 2,
         compiler_params=pltpu.CompilerParams(
-            collective_id=0, has_side_effects=True, vmem_limit_bytes=60 * 2**20),
+            collective_id=0, has_side_effects=True, vmem_limit_bytes=36 * 2**20),
         name="reduced_factors",
     )(slab, test_matrix)
 
 
-def basis_kernel(root, sketch_ref, lower_ref, inverse_ref, proj_ref, basis_ref, coef_ref, factor_ref):
-    @pl.when(pl.program_id(0) == 0)
-    def _():
-        coef_ref[...] = mul(inverse_ref[...], proj_ref[0])
-        factor_ref[...] = lower_ref[...] * F32(1.0 / root)
-
-    basis_ref[...] = mul(sketch_ref[...], inverse_ref[...] * F32(root), NT)
-
-
-def outputs(sketch, lower, inverse, proj, root):
+def basis_kernel(
+    root, sketch_ref, lower_ref, inverse_ref, left_ref, right_ref, basis_hbm, coef_ref, factor_ref, basis, sem
+):
+    inverse = inverse_ref[...]
+    turned = inverse.T * F32(root)
+    copies = []
+    for index in range(CHUNKS):
+        rows = pl.ds(index * CHUNK, CHUNK)
+        basis[rows, :] = mul(sketch_ref[rows, :], turned)
+        copies.append(pltpu.make_async_copy(basis.at[rows], basis_hbm.at[rows], sem.at[index]))
+        copies[-1].start()
+    coef_ref[:, :512] = mul(inverse, left_ref[0])
+    coef_ref[:, 512:] = mul(inverse, right_ref[0])
+    factor_ref[...] = lower_ref[...] * F32(1.0 / root)
+    for copy in copies:
+        copy.wait()
+
+
+def outputs(sketch, lower, inverse, left, right, root):
     rows = sketch.shape[0]
-    square = pl.BlockSpec((256, 256), lambda i: (0, 0))
+    vmem = pl.BlockSpec(memory_space=pltpu.VMEM)
     return pl.pallas_call(
         functools.partial(basis_kernel, root),
-        grid=(rows // CHUNK,),
         out_shape=(
             jax.ShapeDtypeStruct((rows, 256), F32),
             jax.ShapeDtypeStruct((256, 1024), F32),
             jax.ShapeDtypeStruct((256, 256), F32),
         ),
-        in_specs=[
-            pl.BlockSpec((CHUNK, 256), lambda i: (i, 0)),
-            square,
-            square,
-            pl.BlockSpec((1, 256, 1024), lambda i: (0, 0, 0)),
-        ],
-        out_specs=(
-            pl.BlockSpec((CHUNK, 256), lambda i: (i, 0)),
-            pl.BlockSpec((256, 1024), lambda i: (0, 0)),
-            square,
-        ),
-        compiler_params=pltpu.CompilerParams(vmem_limit_bytes=60 * 2**20),
+        in_specs=[vmem] * 5,
+        out_specs=(pl.BlockSpec(memory_space=pl.ANY), vmem, vmem),
+        scratch_shapes=[pltpu.VMEM((rows, 256), F32), pltpu.SemaphoreType.DMA((CHUNKS,))],
+        compiler_params=pltpu.CompilerParams(vmem_limit_bytes=14 * 2**20),
         name="outputs",
-    )(sketch, lower, inverse, proj)
+    )(sketch, lower, inverse, left, right)
 
 
 def local(slab, test_matrix):
     root = float((lax.axis_size("rows") * slab.shape[0]) ** 0.5)
-    sketch, lower, inverse, proj = reduced_factors(slab, test_matrix)
-    return outputs(sketch, lower, inverse, proj, root)
+    sketch, lower, inverse, left, right = reduced_factors(slab, test_matrix)
+    return outputs(sketch, lower, inverse, left, right, root)
 
 
 def solution(mesh):

time: 83.1 us -> 72.5 us (0.87)
  Pallas kernels: 82.1 us -> 69.8 us
  local copies, waits for them, and re-layouts: 0 us -> 1.03 us
    pallas_call x1, Pallas kernels: 68.1 us -> 59.9 us  [reduced_factors(): pl.pallas_call(main_kernel, out_shape=(jax.ShapeDtypeStruct((rows, 256),...]
    pallas_call x1, Pallas kernels: 14 us -> 9.92 us  [outputs(): pl.pallas_call(functools.partial(basis_kernel, root), out_shape=(jax.Shap...]
    unnamed x0 -> x2, local copies, waits for them, and re-layouts: none -> 1.03 us
where the time goes in v3:
time: 72.5 us; the launch traced here: 71.7 us
  Pallas kernels  69.8 us (96%)
  local copies, waits for them, and re-layouts  1.03 us (1%)
  between operations  0.81 us (1%)
    pallas_call x1, Pallas kernels, reduced_factors(): pl.pallas_call(main_kernel, out_shape=(jax.ShapeDtypeStruct((rows, 256),...  59.9 us
    pallas_call x1, Pallas kernels, outputs(): pl.pallas_call(functools.partial(basis_kernel, root), out_shape=(jax.Shap...  9.92 us

profile of v3, /device:TPU:1, one launch (start us, length us, event | category | flops | bytes accessed | tf_op | source)
XLA Modules:
  0.0 71.7 jit_solution(17196611436622959127)
XLA Ops:
  0.6 0.0 copy-start
  0.6 1.0 %copy-done = bf16[1024,256]{1,0:T(8,128)(2,1)S(1)} copy-done((bf16[1024,256]{1,0:T(8,128)(2,1)S(1)}, bf16[1024,256]{1,0:T(8,128)(2,1)}, u32[]{:S(2)}) %copy-start) | copy-done | bytes 524312
  1.7 59.9 %reduced_factors.1 = (f32[8192,256]{1,0:T(8,128)S(1)}, f32[256,256]{1,0:T(8,128)S(1)}, f32[256,256]{1,0:T(8,128)S(1)}, f32[1,256,512]{2,1,0:T(8,128)S(1)}, f32[1,256,512]{2,1,0:T(8,128)S(1)}) custom-call(bf16[8192,1024]{1,0:T(8,128)(2,1)} %slab_hbm.1, bf16[1024,256]{1,0:T(8,128)(2,1)S(1)} %copy-done), custom_call_target="tpu_custom_call" | custom-call | tf_op jit(solution)/shard_map/reduced_factors/pallas_call | solution.py:466
  61.6 9.9 %outputs.1 = (f32[8192,256]{1,0:T(8,128)}, f32[256,1024]{1,0:T(8,128)}, f32[256,256]{1,0:T(8,128)}) custom-call(f32[8192,256]{1,0:T(8,128)S(1)} %get-tuple-element.8.sketch_ref, f32[256,256]{1,0:T(8,128)S(1)} %get-tuple-element.9.lower_ref, f32[256,256]{1,0:T(8,128)S(1)} %get-tuple-element.10.inverse_ref, f32[1,256,512]{2,1,0:T(8,128)S(1)} %get-tuple-element.11.left_ref, ...), custom_call_target="tpu_custom_call" | custom-call | tf_op jit(solution)/shard_map/outputs/pallas_call | solution.py:517
Async XLA Ops:
  0.6 1.0 %copy-start = (bf16[1024,256]{1,0:T(8,128)(2,1)S(1)}, bf16[1024,256]{1,0:T(8,128)(2,1)}, u32[]{:S(2)}) copy-start(bf16[1024,256]{1,0:T(8,128)(2,1)} %test_ref.1) | copy-start | bytes 1572868

commit v4 on v3

--- a/solution.py
+++ b/solution.py
@@ -248,7 +248,7 @@
     return jnp.concatenate(tiles, axis=0)
 
 
-def factor_gram(gram_ref, lower_ref, inverse_ref, work, upper, between):
+def factor_gram(gram_ref, lower_ref, inverse_ref, work, upper, between, late):
     n = 256
     high = gram_ref[0]
     row = lax.broadcasted_iota(jnp.int32, (n, n), 0)
@@ -321,6 +321,7 @@
 
     x = half(delta)
     x = lax.fori_loop(0, 3, lambda _, x: half(delta - mul3(x, x, NT)), x)
+    late()
     square = mul3(x, x)
     fourth = mul3(square, square)
     total = first_inverse + mul3(fourth, first_inverse)
@@ -336,8 +337,8 @@
 
 
 def main_kernel(
-    slab_hbm, test_ref, sketch, lower_ref, inverse_ref, left_out, right_out,
-    slab, turned, gram, low, cross, left, right, gram_out, work, upper, load_sem,
+    slab_hbm, test_hbm, sketch, lower_ref, inverse_ref, left_out, right_out,
+    slab, turned, gram, low, cross, left, right, gram_out, work, upper, test_ref, load_sem, test_sem,
     *scratch,
 ):
     place = Place()
@@ -352,6 +353,8 @@
         rows = rows_of(index)
         return pltpu.make_async_copy(slab_hbm.at[rows], slab.at[rows], load_sem.at[index])
 
+    test_copy = pltpu.make_async_copy(test_hbm, test_ref, test_sem.at[0])
+    test_copy.start()
     for index in range(CHUNKS):
         load(index).start()
     place.signal()
@@ -398,6 +401,7 @@
 
         lax.fori_loop(2 * quarter, 2 * quarter + 2, add, 0)
 
+    test_copy.wait()
     done = 0
     for count in GROUPS:
         for index in range(done, done + count):
@@ -414,43 +418,43 @@
     place.wait()
     gram_sum.start_swap()
     project(0)
+    project(1)
     gram_sum.to_plane()
-    project(1)
     project(2)
-    gram_sum.to_line()
     project(3)
     left_sum.start_swap()
+    gram_sum.to_line()
     project(4)
+    project(5)
     gram_sum.back_to_plane()
-    project(5)
     left_sum.to_plane()
     project(6)
-    gram_sum.back_to_mate()
     project(7)
     right_sum.start_swap()
+    gram_sum.back_to_mate()
     left_sum.to_line()
+    right_sum.to_plane()
     gram_sum.finish()
 
     def between(panel):
         @pl.when(panel == 0)
         def _():
-            right_sum.to_plane()
             left_sum.back_to_plane()
 
         @pl.when(panel == 1)
         def _():
             right_sum.to_line()
-            left_sum.back_to_mate()
 
         @pl.when(panel == 2)
         def _():
-            right_sum.back_to_plane()
+            left_sum.back_to_mate()
 
         @pl.when(panel == 3)
         def _():
-            right_sum.back_to_mate()
-
-    factor_gram(gram_out, lower_ref, inverse_ref, work, upper, between)
+            right_sum.back_to_plane()
+
+    factor_gram(
+        gram_out, lower_ref, inverse_ref, work, upper, between, right_sum.back_to_mate)
     left_sum.finish()
     right_sum.finish()
     gram_sum.drain()
@@ -472,7 +476,7 @@
             jax.ShapeDtypeStruct((1, 256, 512), F32),
             jax.ShapeDtypeStruct((1, 256, 512), F32),
         ),
-        in_specs=[anywhere, vmem],
+        in_specs=[anywhere, anywhere],
         out_specs=(vmem,) * 5,
         scratch_shapes=[
             pltpu.VMEM((rows, 1024), jnp.bfloat16),
@@ -485,7 +489,9 @@
             pltpu.VMEM((2, 256, 256), F32),
             pltpu.VMEM((256, 512), F32),
             pltpu.VMEM((256, 256), F32),
+            pltpu.VMEM((1024, 256), jnp.bfloat16),
             pltpu.SemaphoreType.DMA((CHUNKS,)),
+            pltpu.SemaphoreType.DMA((1,)),
         ] + reduction_scratch(256, 2) + reduction_scratch(512, 1) * 2,
         compiler_params=pltpu.CompilerParams(
             collective_id=0, has_side_effects=True, vmem_limit_bytes=36 * 2**20),

time: 72.5 us -> 72.7 us (level)
  Pallas kernels: 69.8 us -> 70.7 us
    pallas_call x1, Pallas kernels: 59.9 us -> 60.8 us  [reduced_factors(): pl.pallas_call(main_kernel, out_shape=(jax.ShapeDtypeStruct((rows, 256),...]
where the time goes in v4:
time: 72.7 us; the launch traced here: 72.6 us
  Pallas kernels  70.7 us (97%)
  local copies, waits for them, and re-layouts  1.03 us (1%)
  between operations  0.81 us (1%)
    pallas_call x1, Pallas kernels, reduced_factors(): pl.pallas_call(main_kernel, out_shape=(jax.ShapeDtypeStruct((rows, 256),...  60.8 us
    pallas_call x1, Pallas kernels, outputs(): pl.pallas_call(functools.partial(basis_kernel, root), out_shape=(jax.Shap...  9.92 us

profile of v4, /device:TPU:1, one launch (start us, length us, event | category | flops | bytes accessed | tf_op | source)
XLA Modules:
  0.0 72.6 jit_solution(2140011083935266812)
XLA Ops:
  0.6 0.0 copy-start
  0.6 1.0 %copy-done = bf16[1024,256]{1,0:T(8,128)(2,1)S(1)} copy-done((bf16[1024,256]{1,0:T(8,128)(2,1)S(1)}, bf16[1024,256]{1,0:T(8,128)(2,1)}, u32[]{:S(2)}) %copy-start) | copy-done | bytes 524312
  1.7 60.8 %reduced_factors.1 = (f32[8192,256]{1,0:T(8,128)S(1)}, f32[256,256]{1,0:T(8,128)S(1)}, f32[256,256]{1,0:T(8,128)S(1)}, f32[1,256,512]{2,1,0:T(8,128)S(1)}, f32[1,256,512]{2,1,0:T(8,128)S(1)}) custom-call(bf16[8192,1024]{1,0:T(8,128)(2,1)} %slab_hbm.1, bf16[1024,256]{1,0:T(8,128)(2,1)S(1)} %copy-done), custom_call_target="tpu_custom_call" | custom-call | tf_op jit(solution)/shard_map/reduced_factors/pallas_call | solution.py:470
  62.5 9.9 %outputs.1 = (f32[8192,256]{1,0:T(8,128)}, f32[256,1024]{1,0:T(8,128)}, f32[256,256]{1,0:T(8,128)}) custom-call(f32[8192,256]{1,0:T(8,128)S(1)} %get-tuple-element.8.sketch_ref, f32[256,256]{1,0:T(8,128)S(1)} %get-tuple-element.9.lower_ref, f32[256,256]{1,0:T(8,128)S(1)} %get-tuple-element.10.inverse_ref, f32[1,256,512]{2,1,0:T(8,128)S(1)} %get-tuple-element.11.left_ref, ...), custom_call_target="tpu_custom_call" | custom-call | tf_op jit(solution)/shard_map/outputs/pallas_call | solution.py:523
Async XLA Ops:
  0.6 1.0 %copy-start = (bf16[1024,256]{1,0:T(8,128)(2,1)S(1)}, bf16[1024,256]{1,0:T(8,128)(2,1)}, u32[]{:S(2)}) copy-start(bf16[1024,256]{1,0:T(8,128)(2,1)} %test_hbm.1) | copy-start | bytes 1572868
